TPU v7x, 32 devices: a whole 2x2x4 slice. The times are simulated.
32 devices in a mesh: lat: 4 (over z), lon: 8 (over y, x, core).
Axes of the slice: x: 2, y: 2, z: 4, core: 2. Of those that a mesh axis runs over, the one named last changes fastest.
Arguments:
- u_wind: float32 [1440, 16, 128], P('lon', 'lat'), may hold values from -6 to 6
- v_wind: float32 [1440, 16, 128], P('lon', 'lat'), may hold values from -6 to 6
- height: float32 [1440, 16, 128], P('lon', 'lat'), may hold values from -6 to 6
- wave_speed: float32 [128], replicated, may hold values from 0.1 to 0.4
- cutoff: int32 [16], replicated, may hold values from 1 to 720, as said below
Outputs:
- u_next: float32 [1440, 16, 128], P('lon', 'lat')
- v_next: float32 [1440, 16, 128], P('lon', 'lat')
- h_next: float32 [1440, 16, 128], P('lon', 'lat')
Inputs may be any that keep to these rules, and one draw needn't show every extreme that they name: `cutoff`: rows 4 to 11, within 45 degrees of the equator, hold 720, which keeps every wavenumber; the other rows hold smaller values, 1 on the two outermost rows.
All inputs are finite; a program needn't handle non-finite values.
Results may differ from a plain program's by a relative error of at most 0.00005.
Values sent between devices are 32-bit elements; how exact they have to be, the bound alone decides.
A program may use at most 64 MiB of HBM per device.

v0:
```python
import math

import jax
import jax.numpy as jnp
from jax import lax
from jax.sharding import PartitionSpec as P

coriolis_rate = 0.25


def extended(block, sides, width, periodic):
    for axis, dim in sides:
        count = lax.axis_size(axis)
        forward = [(i, i + 1) for i in range(count - 1)]
        if periodic:
            forward.append((count - 1, 0))
        backward = [(target, source) for source, target in forward]
        low = lax.ppermute(
            lax.slice_in_dim(block, block.shape[dim] - width, None, axis=dim), axis, forward
        )
        high = lax.ppermute(lax.slice_in_dim(block, 0, width, axis=dim), axis, backward)
        block = jnp.concatenate([low, block, high], axis=dim)
    return block


def tables(points):
    wavenum = jnp.arange(points // 2 + 1, dtype=jnp.int32)
    lon_ids = jnp.arange(points, dtype=jnp.int32)
    phase = wavenum[:, None] * lon_ids[None, :] % points
    angle = phase.astype(jnp.float32) * (2.0 * math.pi / points)
    weight = (
        jnp.where((wavenum == 0) | (wavenum == points // 2), 1.0, 2.0).astype(jnp.float32) / points
    )
    return (jnp.cos(angle), jnp.sin(angle), wavenum, weight)


def shards(u_wind, v_wind, height, wave_speed, cutoff):
    lon_cells, lat_rows, levels = u_wind.shape
    lat_devs = lax.axis_size("lat")
    points = lon_cells * lax.axis_size("lon")
    total_rows = lat_rows * lat_devs
    band_index = lax.axis_index("lat")
    first_row = band_index * lat_rows
    row_ids = first_row + jnp.arange(lat_rows, dtype=jnp.int32)
    latitude = 0.5 * math.pi - (row_ids.astype(jnp.float32) + 0.5) * (math.pi / total_rows)
    cos_lat = jnp.cos(latitude)[:, None]
    sin_lat = jnp.sin(latitude)[:, None]
    stretch = points / (2.0 * total_rows) / cos_lat
    speed_col = wave_speed[None, None, :]
    cos_table, sin_table, wavenum, weight = tables(points)
    cut_own = lax.dynamic_slice_in_dim(cutoff, first_row, lat_rows)

    def tendency(u_now, v_now, h_now):
        east = extended(jnp.stack([u_now, h_now]), (("lon", 1),), 1, True)
        zonal_u = (east[0, 2:, :, :] - east[0, :-2, :, :]) * 0.5
        zonal_h = (east[1, 2:, :, :] - east[1, :-2, :, :]) * 0.5
        north = extended(jnp.stack([v_now * cos_lat, h_now]), (("lat", 2),), 1, False)
        merid_vc = (north[0, :, :-2, :] - north[0, :, 2:, :]) * 0.5
        merid_h = (north[1, :, :-2, :] - north[1, :, 2:, :]) * 0.5
        tend_u = coriolis_rate * sin_lat * v_now - speed_col * (stretch * zonal_h)
        tend_v = -coriolis_rate * sin_lat * u_now - speed_col * merid_h
        tend_h = -speed_col * (stretch * zonal_u + merid_vc / cos_lat)
        return jnp.stack([tend_u, tend_v, tend_h])

    def circles(tend, cut_rows):
        mode_scale = weight[:, None] * (wavenum[:, None] <= cut_rows[None, :]).astype(jnp.float32)
        whole_circles = lax.all_to_all(tend, "lon", split_axis=3, concat_axis=1, tiled=True)
        count, circle_len, columns, level_part = whole_circles.shape
        flat = whole_circles.reshape(count, circle_len, columns * level_part)
        scale_flat = jnp.repeat(mode_scale, level_part, axis=1)
        cos_coef = jnp.einsum("ki,nil->nkl", cos_table, flat, precision=lax.Precision.HIGHEST)
        sin_coef = jnp.einsum("ki,nil->nkl", sin_table, flat, precision=lax.Precision.HIGHEST)
        smooth = jnp.einsum(
            "ki,nkl->nil", cos_table, cos_coef * scale_flat, precision=lax.Precision.HIGHEST
        )
        smooth = smooth + jnp.einsum(
            "ki,nkl->nil", sin_table, sin_coef * scale_flat, precision=lax.Precision.HIGHEST
        )
        smooth = smooth.reshape(count, circle_len, columns, level_part)
        return lax.all_to_all(smooth, "lon", split_axis=1, concat_axis=3, tiled=True)

    def filtered(tend):
        return circles(tend, cut_own)

    fields = (u_wind, v_wind, height)
    change = filtered(tendency(u_wind, v_wind, height))
    first = [fields[n] + change[n] for n in range(3)]
    change = filtered(tendency(first[0], first[1], first[2]))
    second = [0.75 * fields[n] + 0.25 * (first[n] + change[n]) for n in range(3)]
    change = filtered(tendency(second[0], second[1], second[2]))
    third = [1.0 / 3.0 * fields[n] + 2.0 / 3.0 * (second[n] + change[n]) for n in range(3)]
    return (third[0], third[1], third[2])


def solution(mesh):
    in_specs = (P("lon", "lat", None), P("lon", "lat", None), P("lon", "lat", None), P(), P())
    out_specs = (P("lon", "lat", None), P("lon", "lat", None), P("lon", "lat", None))
    return jax.shard_map(shards, mesh=mesh, in_specs=in_specs, out_specs=out_specs, check_vma=False)
```

profile of v0, /device:TPU:0, one launch (start us, length us, event | category | flops | bytes accessed | tf_op | source)
XLA Modules:
  0.0 657.2 jit_solution(3765198613175271260)
XLA Ops:
  8.0 10.1 %collective-permute-done = f32[2,1,4,128]{1,3,2,0:T(8,128)S(1)} collective-permute-done((f32[2,1,4,128]{1,3,2,0:T(8,128)S(1)}, f32[2,1,4,128]{1,3,2,0:T(8,128)S(1)}, u32[]{:S(2)}, u32[]{:S(2)}) %collective-permute-start) | collective-permute-done | bytes 4128 | tf_op jit(solution)/shard_map/ppermute | solution.py:21
  41.4 20.9 %all-to-all-done = f32[3,180,4,128]{1,2,0,3:T(4,128)} async-done(((f32[3,180,4,128]{1,2,0,3:T(4,128)}), f32[3,180,4,128]{1,2,0,3:T(4,128)}, u32[]{:S(2)}, u32[]{:S(2)}) %all-to-all-start) | async-done | bytes 1105952 | tf_op jit(solution)/shard_map/all_to_all | solution.py:67
  68.4 21.2 %fusion.112 = f32[3,721,64]{1,2,0:T(8,128)S(1)} fusion(f32[3,1440,64]{1,2,0:T(8,128)S(1)} %reshape.90, f32[721,64]{0,1:T(8,128)S(1)} %bitcast.264), kind=kOutput, calls=%fused_computation.77 | convolution fusion | flops 2401587456 | bytes 1844224 | tf_op jit(solution)/shard_map/ki,nil->nkl/dot_general | solution.py:72
  89.6 21.2 %fusion.121 = f32[3,721,64]{1,2,0:T(8,128)S(1)} fusion(f32[3,1440,64]{1,2,0:T(8,128)S(1)} %reshape.90, f32[721,64]{0,1:T(8,128)S(1)} %bitcast.265), kind=kOutput, calls=%fused_computation.80 | convolution fusion | flops 2401587456 | bytes 1844224 | tf_op jit(solution)/shard_map/ki,nil->nkl/dot_general | solution.py:71
  110.8 21.9 %fusion.10 = f32[3,64,1440]{2,1,0:T(8,128)S(1)} fusion(f32[3,721,64]{1,2,0:T(8,128)S(1)} %fusion.112), kind=kOutput, calls=%fused_computation.11 | convolution fusion | flops 2401449216 | bytes 1659648 | tf_op jit(solution)/shard_map/ki,nkl->nil/dot_general | solution.py:76
  132.7 22.0 %fusion.43 = f32[3,64,1440]{2,1,0:T(8,128)S(1)} fusion(f32[3,64,1440]{2,1,0:T(8,128)S(1)} %fusion.10, f32[3,721,64]{1,2,0:T(8,128)S(1)} %fusion.121), kind=kOutput, calls=%fused_computation.33 | convolution fusion | flops 2401725696 | bytes 2765568 | tf_op jit(solution)/shard_map/ki,nkl->nil/dot_general | solution.py:73
  161.6 10.4 %reshape.98 = f32[8,1,34560]{2,1,0:T(1,128)} reshape(f32[1440,3,4,16]{3,2,1,0:T(4,128)} %bitcast.231) | data formatting | bytes 2211840
  172.1 19.9 %all_to_all.90 = f32[8,1,34560]{2,1,0:T(1,128)S(1)} all-to-all(f32[8,1,34560]{2,1,0:T(1,128)} %reshape.98), channel_id=1, replica_groups=mesh['lat'=4,'lon'=8] {'lon'}, dimensions={0} | all-to-all | bytes 2211840 | tf_op jit(solution)/shard_map/all_to_all | solution.py:80
  197.1 10.7 %reshape.99 = f32[1440,3,4,16]{3,2,1,0:T(4,128)} reshape(f32[8,34560]{1,0:T(8,128)} %reduce) | data formatting | bytes 2211840
  207.8 8.2 %copy.101 = f32[3,8,180,4,16]{2,1,4,3,0:T(8,128)} copy(f32[3,8,180,4,16]{4,3,0,2,1:T(4,128)} %bitcast.228) | data formatting | bytes 2211840 | tf_op jit(solution)/shard_map/all_to_all | solution.py:80
  219.0 10.9 %collective-permute-done.4 = f32[2,1,4,128]{1,3,2,0:T(8,128)S(1)} collective-permute-done((f32[2,1,4,128]{1,3,2,0:T(8,128)S(1)}, f32[2,1,4,128]{1,3,2,0:T(8,128)S(1)}, u32[]{:S(2)}, u32[]{:S(2)}) %collective-permute-start.4) | collective-permute-done | bytes 4128 | tf_op jit(solution)/shard_map/ppermute | solution.py:21
  247.4 24.3 %all_to_all.91 = f32[3,180,4,128]{1,2,0,3:T(4,128)S(1)} all-to-all(f32[3,180,4,128]{1,2,0,3:T(4,128)S(1)} %copy.78), channel_id=1, replica_groups=mesh['lat'=4,'lon'=8] {'lon'}, dimensions={3} | all-to-all | bytes 2211840 | tf_op jit(solution)/shard_map/all_to_all | solution.py:67
  277.2 22.5 %fusion.109 = f32[3,721,64]{1,2,0:T(8,128)S(1)} fusion(f32[3,1440,64]{1,2,0:T(8,128)} %reshape.92, f32[721,64]{0,1:T(8,128)S(1)} %bitcast.266), kind=kOutput, calls=%fused_computation.76 | convolution fusion | flops 2401587456 | bytes 1844224 | tf_op jit(solution)/shard_map/ki,nil->nkl/dot_general | solution.py:72
  299.8 21.3 %fusion.118 = f32[3,721,64]{1,2,0:T(8,128)S(1)} fusion(f32[3,1440,64]{1,2,0:T(8,128)S(1)} %copy-done.7, f32[721,64]{0,1:T(8,128)S(1)} %bitcast.267), kind=kOutput, calls=%fused_computation.79 | convolution fusion | flops 2401587456 | bytes 1844224 | tf_op jit(solution)/shard_map/ki,nil->nkl/dot_general | solution.py:71
  321.0 22.1 %fusion.6 = f32[3,64,1440]{2,1,0:T(8,128)S(1)} fusion(f32[3,721,64]{1,2,0:T(8,128)S(1)} %fusion.109), kind=kOutput, calls=%fused_computation.7 | convolution fusion | flops 2401449216 | bytes 1659648 | tf_op jit(solution)/shard_map/ki,nkl->nil/dot_general | solution.py:76
  343.2 24.3 %fusion.46 = f32[3,64,1440]{2,1,0:T(8,128)} fusion(f32[3,64,1440]{2,1,0:T(8,128)S(1)} %fusion.6, f32[3,721,64]{1,2,0:T(8,128)S(1)} %fusion.118), kind=kOutput, calls=%fused_computation.34 | convolution fusion | flops 2401725696 | bytes 2765568 | tf_op jit(solution)/shard_map/ki,nkl->nil/dot_general | solution.py:73
  367.5 8.4 %copy.81 = f32[3,1440,4,16]{3,2,0,1:T(4,128)} copy(f32[3,1440,4,16]{1,3,2,0:T(8,128)} %bitcast.262) | data formatting | bytes 2211840 | tf_op jit(solution)/shard_map/reshape | solution.py:79
  375.8 10.6 %reshape.100 = f32[8,1,34560]{2,1,0:T(1,128)} reshape(f32[1440,3,4,16]{3,2,1,0:T(4,128)} %bitcast.232) | data formatting | bytes 2211840
  386.4 20.2 %all_to_all.92 = f32[8,1,34560]{2,1,0:T(1,128)} all-to-all(f32[8,1,34560]{2,1,0:T(1,128)} %reshape.100), channel_id=1, replica_groups=mesh['lat'=4,'lon'=8] {'lon'}, dimensions={0} | all-to-all | bytes 2211840 | tf_op jit(solution)/shard_map/all_to_all | solution.py:80
  412.1 10.7 %reshape.101 = f32[1440,3,4,16]{3,2,1,0:T(4,128)} reshape(f32[8,34560]{1,0:T(8,128)} %reduce.1) | data formatting | bytes 2211840
  422.9 8.2 %copy.102 = f32[3,8,180,4,16]{2,1,4,3,0:T(8,128)} copy(f32[3,8,180,4,16]{4,3,0,2,1:T(4,128)} %bitcast.229) | data formatting | bytes 2211840 | tf_op jit(solution)/shard_map/all_to_all | solution.py:80
  434.5 10.9 %collective-permute-done.8 = f32[2,1,4,128]{1,3,2,0:T(8,128)S(1)} collective-permute-done((f32[2,1,4,128]{1,3,2,0:T(8,128)S(1)}, f32[2,1,4,128]{1,3,2,0:T(8,128)S(1)}, u32[]{:S(2)}, u32[]{:S(2)}) %collective-permute-start.8) | collective-permute-done | bytes 4128 | tf_op jit(solution)/shard_map/ppermute | solution.py:21
  463.0 24.3 %all_to_all.93 = f32[3,180,4,128]{1,2,0,3:T(4,128)S(1)} all-to-all(f32[3,180,4,128]{1,2,0,3:T(4,128)S(1)} %copy.88), channel_id=1, replica_groups=mesh['lat'=4,'lon'=8] {'lon'}, dimensions={3} | all-to-all | bytes 2211840 | tf_op jit(solution)/shard_map/all_to_all | solution.py:67
  492.8 22.5 %fusion.106 = f32[3,721,64]{1,2,0:T(8,128)S(1)} fusion(f32[3,1440,64]{1,2,0:T(8,128)} %reshape.94, f32[721,64]{0,1:T(8,128)S(1)} %bitcast.268), kind=kOutput, calls=%fused_computation.75 | convolution fusion | flops 2401587456 | bytes 1844224 | tf_op jit(solution)/shard_map/ki,nil->nkl/dot_general | solution.py:72
  515.4 21.5 %fusion.115 = f32[3,721,64]{1,2,0:T(8,128)S(1)} fusion(f32[3,1440,64]{1,2,0:T(8,128)S(1)} %copy-done.6, f32[721,64]{0,1:T(8,128)S(1)} %bitcast.269), kind=kOutput, calls=%fused_computation.78 | convolution fusion | flops 2401587456 | bytes 1844224 | tf_op jit(solution)/shard_map/ki,nil->nkl/dot_general | solution.py:71
  536.8 21.9 %fusion.2 = f32[3,64,1440]{2,1,0:T(8,128)S(1)} fusion(f32[3,721,64]{1,2,0:T(8,128)S(1)} %fusion.106), kind=kOutput, calls=%fused_computation.3 | convolution fusion | flops 2401449216 | bytes 1659648 | tf_op jit(solution)/shard_map/ki,nkl->nil/dot_general | solution.py:76
  558.7 24.3 %fusion.49 = f32[3,64,1440]{2,1,0:T(8,128)} fusion(f32[3,64,1440]{2,1,0:T(8,128)S(1)} %fusion.2, f32[3,721,64]{1,2,0:T(8,128)S(1)} %fusion.115), kind=kOutput, calls=%fused_computation.35 | convolution fusion | flops 2401725696 | bytes 2765568 | tf_op jit(solution)/shard_map/ki,nkl->nil/dot_general | solution.py:73
  583.0 8.4 %copy.91 = f32[3,1440,4,16]{3,2,0,1:T(4,128)} copy(f32[3,1440,4,16]{1,3,2,0:T(8,128)} %bitcast.263) | data formatting | bytes 2211840 | tf_op jit(solution)/shard_map/reshape | solution.py:79
  591.4 10.6 %reshape.102 = f32[8,1,34560]{2,1,0:T(1,128)} reshape(f32[1440,3,4,16]{3,2,1,0:T(4,128)} %bitcast.233) | data formatting | bytes 2211840
  602.0 20.2 %all_to_all.94 = f32[8,1,34560]{2,1,0:T(1,128)} all-to-all(f32[8,1,34560]{2,1,0:T(1,128)} %reshape.102), channel_id=1, replica_groups=mesh['lat'=4,'lon'=8] {'lon'}, dimensions={0} | all-to-all | bytes 2211840 | tf_op jit(solution)/shard_map/all_to_all | solution.py:80
  627.7 10.7 %reshape.103 = f32[1440,3,4,16]{3,2,1,0:T(4,128)} reshape(f32[8,34560]{1,0:T(8,128)} %reduce.2) | data formatting | bytes 2211840
  638.5 8.2 %copy.103 = f32[3,8,180,4,16]{2,1,4,3,0:T(8,128)} copy(f32[3,8,180,4,16]{4,3,0,2,1:T(4,128)} %bitcast.230) | data formatting | bytes 2211840 | tf_op jit(solution)/shard_map/all_to_all | solution.py:80
  (115 shorter events, 122.1 us)
Async XLA Ops:
  0.6 21.0 %copy-start.8 = (f32[128]{0:T(128)S(1)}, f32[128]{0:T(128)}, u32[]{:S(2)}) copy-start(f32[128]{0:T(128)} %param.8) | copy-start | bytes 1540
  3.2 14.8 %collective-permute-start = (f32[2,1,4,128]{1,3,2,0:T(8,128)S(1)}, f32[2,1,4,128]{1,3,2,0:T(8,128)S(1)}, u32[]{:S(2)}, u32[]{:S(2)}) collective-permute-start(f32[2,1,4,128]{1,3,2,0:T(8,128)S(1)} %get-tuple-element.39), channel_id=1, source_target_pairs={{1,0},{2,1},{3,2},{4,3},{5,4},{6,5},{7,6},{0,7},{9,8},{10,9},{11,1... | collective-permute-start | bytes 12296 | tf_op jit(solution)/shard_map/ppermute | solution.py:21
  6.6 13.4 %collective-permute-start.1 = (f32[2,1,4,128]{1,3,2,0:T(8,128)S(1)}, f32[2,1,4,128]{1,3,2,0:T(8,128)}, u32[]{:S(2)}, u32[]{:S(2)}) collective-permute-start(f32[2,1,4,128]{1,3,2,0:T(8,128)S(1)} %get-tuple-element.40), channel_id=1, source_target_pairs={{0,1},{1,2},{2,3},{3,4},{4,5},{5,6},{6,7},{7,0},{8,9},{9,10},{10,1... | collective-permute-start | bytes 12296 | tf_op jit(solution)/shard_map/ppermute | solution.py:18
  21.9 7.4 %collective-permute-start.2 = (f32[2,180,1,128]{1,3,2,0:T(8,128)S(1)}, f32[2,180,1,128]{1,3,2,0:T(8,128)S(1)}, u32[]{:S(2)}, u32[]{:S(2)}) collective-permute-start(f32[2,180,1,128]{1,3,2,0:T(8,128)S(1)} %get-tuple-element.41), channel_id=1, source_target_pairs={{0,8},{8,16},{16,24},{1,9},{9,17},{17,25},{2,10},{10,18},{18,26},{... | collective-permute-start | bytes 552968 | tf_op jit(solution)/shard_map/ppermute | solution.py:18
  25.4 8.3 %collective-permute-start.3 = (f32[2,180,1,128]{1,3,2,0:T(8,128)S(1)}, f32[2,180,1,128]{1,3,2,0:T(8,128)S(1)}, u32[]{:S(2)}, u32[]{:S(2)}) collective-permute-start(f32[2,180,1,128]{1,3,2,0:T(8,128)S(1)} %get-tuple-element.42), channel_id=1, source_target_pairs={{8,0},{16,8},{24,16},{9,1},{17,9},{25,17},{10,2},{18,10},{26,18},{... | collective-permute-start | bytes 552968 | tf_op jit(solution)/shard_map/ppermute | solution.py:21
  34.1 7.2 %copy-start.9 = (s32[16]{0:T(128)S(1)}, s32[16]{0:T(128)}, u32[]{:S(2)}) copy-start(s32[16]{0:T(128)} %param.9) | copy-start | bytes 196
  36.4 25.9 %all-to-all-start = ((f32[3,180,4,128]{1,2,0,3:T(4,128)}), f32[3,180,4,128]{1,2,0,3:T(4,128)}, u32[]{:S(2)}, u32[]{:S(2)}) async-start(f32[3,180,4,128]{1,2,0,3:T(4,128)} %copy.67), calls=%async_computation | async-start | bytes 3145728 | tf_op jit(solution)/shard_map/all_to_all | solution.py:67
  218.2 11.7 %collective-permute-start.4 = (f32[2,1,4,128]{1,3,2,0:T(8,128)S(1)}, f32[2,1,4,128]{1,3,2,0:T(8,128)S(1)}, u32[]{:S(2)}, u32[]{:S(2)}) collective-permute-start(f32[2,1,4,128]{1,3,2,0:T(8,128)S(1)} %get-tuple-element.35), channel_id=1, source_target_pairs={{1,0},{2,1},{3,2},{4,3},{5,4},{6,5},{7,6},{0,7},{9,8},{10,9},{11,1... | collective-permute-start | bytes 12296 | tf_op jit(solution)/shard_map/ppermute | solution.py:21
  218.3 14.2 %collective-permute-start.5 = (f32[2,1,4,128]{1,3,2,0:T(8,128)S(1)}, f32[2,1,4,128]{1,3,2,0:T(8,128)S(1)}, u32[]{:S(2)}, u32[]{:S(2)}) collective-permute-start(f32[2,1,4,128]{1,3,2,0:T(8,128)S(1)} %get-tuple-element.36), channel_id=1, source_target_pairs={{0,1},{1,2},{2,3},{3,4},{4,5},{5,6},{6,7},{7,0},{8,9},{9,10},{10,1... | collective-permute-start | bytes 12296 | tf_op jit(solution)/shard_map/ppermute | solution.py:18
  233.4 12.9 %copy-start.2 = (f32[180,4,128]{0,2,1:T(8,128)}, f32[180,4,128]{0,2,1:T(8,128)S(1)}, u32[]{:S(2)}) copy-start(f32[180,4,128]{0,2,1:T(8,128)S(1)} %get-tuple-element.15) | copy-start | bytes 1105924
  233.5 8.2 %collective-permute-start.6 = (f32[2,180,1,128]{1,3,2,0:T(8,128)S(1)}, f32[2,180,1,128]{1,3,2,0:T(8,128)S(1)}, u32[]{:S(2)}, u32[]{:S(2)}) collective-permute-start(f32[2,180,1,128]{1,3,2,0:T(8,128)S(1)} %get-tuple-element.31), channel_id=1, source_target_pairs={{0,8},{8,16},{16,24},{1,9},{9,17},{17,25},{2,10},{10,18},{18,26},{... | collective-permute-start | bytes 552968 | tf_op jit(solution)/shard_map/ppermute | solution.py:18
  237.0 8.8 %collective-permute-start.7 = (f32[2,180,1,128]{1,3,2,0:T(8,128)S(1)}, f32[2,180,1,128]{1,3,2,0:T(8,128)S(1)}, u32[]{:S(2)}, u32[]{:S(2)}) collective-permute-start(f32[2,180,1,128]{1,3,2,0:T(8,128)S(1)} %get-tuple-element.32), channel_id=1, source_target_pairs={{8,0},{16,8},{24,16},{9,1},{17,9},{25,17},{10,2},{18,10},{26,18},{... | collective-permute-start | bytes 552968 | tf_op jit(solution)/shard_map/ppermute | solution.py:21
  277.2 22.5 %copy-start.7 = (f32[3,1440,64]{1,2,0:T(8,128)S(1)}, f32[3,1440,64]{1,2,0:T(8,128)}, u32[]{:S(2)}) copy-start(f32[3,1440,64]{1,2,0:T(8,128)} %reshape.92) | copy-start | bytes 3317764
  432.8 0.8 copy-start
  433.1 15.6 %copy-start.3 = (f32[180,4,128]{0,2,1:T(8,128)S(1)}, f32[180,4,128]{0,2,1:T(8,128)}, u32[]{:S(2)}) copy-start(f32[180,4,128]{0,2,1:T(8,128)} %copy-done.2) | copy-start | bytes 1105924
  433.8 11.7 %collective-permute-start.8 = (f32[2,1,4,128]{1,3,2,0:T(8,128)S(1)}, f32[2,1,4,128]{1,3,2,0:T(8,128)S(1)}, u32[]{:S(2)}, u32[]{:S(2)}) collective-permute-start(f32[2,1,4,128]{1,3,2,0:T(8,128)S(1)} %get-tuple-element.29), channel_id=1, source_target_pairs={{1,0},{2,1},{3,2},{4,3},{5,4},{6,5},{7,6},{0,7},{9,8},{10,9},{11,1... | collective-permute-start | bytes 12296 | tf_op jit(solution)/shard_map/ppermute | solution.py:21
  433.9 14.2 %collective-permute-start.9 = (f32[2,1,4,128]{1,3,2,0:T(8,128)S(1)}, f32[2,1,4,128]{1,3,2,0:T(8,128)S(1)}, u32[]{:S(2)}, u32[]{:S(2)}) collective-permute-start(f32[2,1,4,128]{1,3,2,0:T(8,128)S(1)} %get-tuple-element.30), channel_id=1, source_target_pairs={{0,1},{1,2},{2,3},{3,4},{4,5},{5,6},{6,7},{7,0},{8,9},{9,10},{10,1... | collective-permute-start | bytes 12296 | tf_op jit(solution)/shard_map/ppermute | solution.py:18
  448.9 12.9 %copy-start.4 = (f32[180,4,128]{0,2,1:T(8,128)}, f32[180,4,128]{0,2,1:T(8,128)S(1)}, u32[]{:S(2)}) copy-start(f32[180,4,128]{0,2,1:T(8,128)S(1)} %get-tuple-element.13) | copy-start | bytes 1105924
  449.1 8.2 %collective-permute-start.10 = (f32[2,180,1,128]{1,3,2,0:T(8,128)S(1)}, f32[2,180,1,128]{1,3,2,0:T(8,128)S(1)}, u32[]{:S(2)}, u32[]{:S(2)}) collective-permute-start(f32[2,180,1,128]{1,3,2,0:T(8,128)S(1)} %get-tuple-element.25), channel_id=1, source_target_pairs={{0,8},{8,16},{16,24},{1,9},{9,17},{17,25},{2,10},{10,18},{18,26},{... | collective-permute-start | bytes 552968 | tf_op jit(solution)/shard_map/ppermute | solution.py:18
  452.6 8.8 %collective-permute-start.11 = (f32[2,180,1,128]{1,3,2,0:T(8,128)S(1)}, f32[2,180,1,128]{1,3,2,0:T(8,128)S(1)}, u32[]{:S(2)}, u32[]{:S(2)}) collective-permute-start(f32[2,180,1,128]{1,3,2,0:T(8,128)S(1)} %get-tuple-element.26), channel_id=1, source_target_pairs={{8,0},{16,8},{24,16},{9,1},{17,9},{25,17},{10,2},{18,10},{26,18},{... | collective-permute-start | bytes 552968 | tf_op jit(solution)/shard_map/ppermute | solution.py:21
  492.8 22.5 %copy-start.6 = (f32[3,1440,64]{1,2,0:T(8,128)S(1)}, f32[3,1440,64]{1,2,0:T(8,128)}, u32[]{:S(2)}) copy-start(f32[3,1440,64]{1,2,0:T(8,128)} %reshape.94) | copy-start | bytes 3317764
  646.7 2.7 copy-start.1
  650.4 5.4 copy-start.5
where the time goes:
time: 663 us; the launch traced here: 657 us
  matrix products  267 us (40%)
  local copies, waits for them, and re-layouts  150 us (23%)
  blocking collectives  109 us (16%)
  waiting for transfers between devices  81.8 us (12%)
  other arithmetic  24.3 us (4%)
  starting transfers between devices  24.1 us (4%)
    unnamed x32, local copies, waits for them, and re-layouts  71.8 us
    dot_general x3, matrix products, circles(): jnp.einsum('ki,nkl->nil', cos_table, cos_coef * scale_flat, precision=lax...  70.6 us
    dot_general x3, matrix products, circles(): jnp.einsum('ki,nil->nkl', sin_table, flat, precision=lax.Precision.HIGHEST)  66.2 us
    dot_general x3, matrix products, circles(): jnp.einsum('ki,nkl->nil', sin_table, sin_coef * scale_flat, precision=lax...  66 us
    dot_general x3, matrix products, circles(): jnp.einsum('ki,nil->nkl', cos_table, flat, precision=lax.Precision.HIGHEST)  64 us
    all_to_all x3, blocking collectives, circles(): lax.all_to_all(smooth, 'lon', split_axis=1, concat_axis=3, tiled=True)  60.3 us
    all_to_all x2, blocking collectives, circles(): lax.all_to_all(tend, 'lon', split_axis=3, concat_axis=1, tiled=True)  48.7 us
    ppermute x6, waiting for transfers between devices, extended(): lax.ppermute(lax.slice_in_dim(block, 0, width, axis=dim), axis, backward)  44.6 us
  transfers between devices with their start and end apart: 13, of which 13 were waited for; matrix products, arithmetic and copies ran while one was open for 0% of the time, Pallas kernels for 0%

commit v1 on v0

v1 whole, which is shorter than its diff:
```python
import functools
import math

import jax
import jax.numpy as jnp
import numpy as np
from jax import lax
from jax.experimental import pallas as pl
from jax.experimental.pallas import tpu as pltpu
from jax.sharding import PartitionSpec as P

coriolis_rate = 0.25
MESH = pl.DeviceIdType.MESH
RADIX = 8
ROOT = math.sqrt(0.5)


def round_up(value, unit):
    return -(-value // unit) * unit


def widened(table):
    hi = table.astype(jnp.bfloat16)
    lo = (table - hi.astype(np.float64)).astype(jnp.bfloat16)
    return np.concatenate([hi, hi, lo], axis=-1)


def tables(points, cells, pad_cells):
    part = points // RADIX
    subs = part // cells
    pad = subs * pad_cells
    place = np.concatenate([np.arange(cells) + j * pad_cells for j in range(subs)])
    spots = np.arange(part)
    unit = 2.0 * np.pi / points

    def placed(block):
        out = np.zeros((pad, pad))
        out[: block.shape[0], place] = block
        return out

    half = part // 2
    q = np.arange(half + 1)
    even = (RADIX * q)[:, None] * spots[None, :] % points * unit
    scale = np.where((q == 0) | (q == half), 1.0, 2.0)[:, None]
    first = np.concatenate(
        [np.cos(even) * np.sqrt(scale / points), np.sin(even[1:half]) * np.sqrt(2.0 / points)]
    )
    q = np.arange(half)
    odd = (RADIX * q + RADIX // 2)[:, None] * spots[None, :] % points * unit
    last = np.concatenate([np.cos(odd), np.sin(odd)]) * np.sqrt(2.0 / points)
    real = np.stack([placed(first), placed(last)])
    mixed = []
    for s in (1, 2, 3):
        q = np.arange(part)
        angle = (RADIX * q + s)[:, None] * spots[None, :] % points * unit
        c, d = placed(np.cos(angle)), placed(np.sin(angle))
        mixed.append(np.block([[c, d], [-d, c]]) * np.sqrt(2.0 / points))
    mixed = np.stack(mixed)
    return tuple(
        np.stack([widened(table), widened(np.swapaxes(table, 1, 2))]) for table in (real, mixed)
    )


def geometry(points, bands, rows, width):
    total = rows * bands
    latitude = 0.5 * np.pi - (np.arange(total) + 0.5) * (np.pi / total)
    out = []
    for band in range(bands):
        own = latitude[band * rows : (band + 1) * rows]
        cos_lat, sin_lat = np.repeat(np.cos(own), width), np.repeat(np.sin(own), width)
        stretch = points / (2.0 * total) / cos_lat
        zero, one = np.zeros_like(cos_lat), np.ones_like(cos_lat)
        pairs = (
            (0.5 * stretch, 0.5 * one),
            (0.5 * stretch, zero),
            (0.5 / cos_lat, zero),
            (coriolis_rate * sin_lat, -coriolis_rate * sin_lat),
            (zero, cos_lat),
            (zero, zero),
            (zero, zero),
            (zero, zero),
        )
        out.extend(np.concatenate(pair) for pair in pairs)
    return np.stack(out).astype(np.float32)


def roll(value, shift):
    width = value.shape[-1]
    shift = shift % width
    if shift == 0:
        return value
    if width == 128:
        return pltpu.roll(value, shift, 1)
    return jnp.concatenate([value[:, width - shift :], value[:, : width - shift]], axis=1)


def dot(a, b):
    return jnp.dot(a, b, preferred_element_type=jnp.float32)


def split(value):
    hi = value.astype(jnp.bfloat16)
    return hi, (value - hi.astype(jnp.float32)).astype(jnp.bfloat16)


def kernel(
    dims,
    u_hbm,
    v_hbm,
    h_hbm,
    speed_hbm,
    cutoff_ref,
    geo_hbm,
    real_hbm,
    mixed_hbm,
    u_out,
    v_out,
    h_out,
    u_ref,
    v_ref,
    h_ref,
    speed_ref,
    geo_ref,
    real_t,
    mixed_t,
    send1,
    recv1,
    send2,
    recv2,
    base_uv,
    base_h,
    cur_uv,
    cur_h,
    tend_uv,
    tend_h,
    y_in,
    y_out,
    halo_send,
    halo_recv,
    table_sem,
    send1_sem,
    recv1_sem,
    send2_sem,
    recv2_sem,
    hsend_sem,
    hrecv_sem,
):
    bands, devs, cells, rows, width, pad, wire, half = dims
    points = cells * devs
    part = points // RADIX
    subs = devs // RADIX
    part_pad = subs * pad
    span = rows * width
    slab = 2 * span
    levels = width * devs
    me = lax.axis_index("lon")
    band = lax.axis_index("lat")
    has_north = band > 0
    has_south = band < bands - 1

    local = [
        pltpu.make_async_copy(source, target, table_sem.at[n])
        for n, (source, target) in enumerate(
            (
                (u_hbm, u_ref),
                (v_hbm, v_ref),
                (h_hbm, h_ref),
                (speed_hbm, speed_ref),
                (geo_hbm, geo_ref),
                (real_hbm, real_t),
                (mixed_hbm, mixed_t),
            )
        )
    ]
    for copy in local:
        copy.start()

    barrier = pltpu.get_barrier_semaphore()

    def greet(k, _):
        pl.semaphore_signal(
            barrier, inc=1, device_id={"lon": lax.rem(me + k, devs)}, device_id_type=MESH
        )
        return 0

    lax.fori_loop(1, devs, greet, 0)

    @pl.when(has_north)
    def _():
        pl.semaphore_signal(barrier, inc=1, device_id={"lat": band - 1}, device_id_type=MESH)

    @pl.when(has_south)
    def _():
        pl.semaphore_signal(barrier, inc=1, device_id={"lat": band + 1}, device_id_type=MESH)

    pl.semaphore_wait(
        barrier, devs - 1 + has_north.astype(jnp.int32) + has_south.astype(jnp.int32)
    )

    for copy in local[:3]:
        copy.wait()

    lane_lev = lax.broadcasted_iota(jnp.int32, (cells, levels), 1)
    fields = (u_ref, v_ref, h_ref)
    uv_units = [(fields[n // rows], n % rows, 0) for n in range(2 * rows)]
    h_units = [(h_ref, n % rows, (n // rows) * (cells - half)) for n in range(2 * rows)]

    def packed(units, count, peer):
        total = jnp.zeros((count, levels), jnp.float32)
        lane = lane_lev[:count]
        for n, (ref, row, start) in enumerate(units):
            piece = ref[pl.ds(row + rows * start, count, stride=rows), :]
            shift = lax.rem(n * width - peer * width + levels, levels)
            piece = pltpu.roll(piece, shift, 1)
            total = jnp.where((lane >= n * width) & (lane < (n + 1) * width), piece, total)
        return total[:, :slab]

    def fill(target, slot, peer):
        target[slot, wire - 8 : wire, :] = jnp.zeros((8, slab), jnp.float32)
        target[slot, 0:cells, :] = packed(uv_units, cells, peer)
        target[slot, wire : wire + half, :] = packed(h_units, half, peer)

    def copy1(peer, index):
        return pltpu.make_async_remote_copy(
            src_ref=send1.at[peer],
            dst_ref=recv1.at[index],
            send_sem=send1_sem.at[peer],
            recv_sem=recv1_sem.at[index],
            device_id={"lon": peer},
            device_id_type=MESH,
        )

    def copy2(peer, index):
        return pltpu.make_async_remote_copy(
            src_ref=send2.at[peer],
            dst_ref=recv2.at[index],
            send_sem=send2_sem.at[peer],
            recv_sem=recv2_sem.at[index],
            device_id={"lon": peer},
            device_id_type=MESH,
        )

    def out1(k, _):
        peer = lax.rem(me + k, devs)
        fill(send1, peer, peer)
        copy1(peer, me).start()
        return 0

    lax.fori_loop(1, devs, out1, 0)
    fill(recv1, me, me)

    for copy in local[3:5]:
        copy.wait()
    lane = lax.broadcasted_iota(jnp.int32, (1, slab), 1)
    low = lane < span
    groups = devs // 4
    my_group = me // 4
    all_speeds = jnp.broadcast_to(speed_ref[...], (8, levels))
    own_first = pltpu.roll(all_speeds, lax.rem(levels - me * width, levels), 1)
    lane8 = lax.broadcasted_iota(jnp.int32, (8, levels), 1)
    speed = jnp.zeros((8, levels), jnp.float32)
    cut = jnp.zeros((1, slab), jnp.float32)
    for n in range(2 * rows):
        moved = pltpu.roll(own_first, n * width, 1) if n else own_first
        speed = jnp.where((lane8 >= n * width) & (lane8 < (n + 1) * width), moved, speed)
        row_cut = cutoff_ref[band * rows + n % rows].astype(jnp.float32)
        cut = jnp.where((lane >= n * width) & (lane < (n + 1) * width), row_cut, cut)
    cut = jnp.concatenate([cut, cut], axis=1)
    geo = geo_ref[pl.ds(pl.multiple_of(band * 8, 8), 8), :]
    scaled = geo * speed[:, :slab]
    k1, k2, k3 = scaled[0:1], scaled[1:2], scaled[2:3]
    fcor, cosl = geo[3:4], geo[4:5]

    @pl.when(band == 0)
    def _():
        for t in range(3):
            halo_recv[t, 0] = jnp.zeros(halo_recv.shape[2:], jnp.float32)

    @pl.when(band == bands - 1)
    def _():
        for t in range(3):
            halo_recv[t, 1] = jnp.zeros(halo_recv.shape[2:], jnp.float32)

    def unpack(b):
        uv = recv1[b, 0:wire, :]
        hp = recv1[b, wire : wire + half, :]
        other = roll(hp, span)
        for buf_uv, buf_h, at in ((base_uv, base_h, 0), (cur_uv, cur_h, 8)):
            zeros = jnp.zeros((16, slab), jnp.float32)
            buf_uv[b, at + pad - 16 : at + pad, :] = zeros
            buf_h[b, at + pad - 16 : at + pad, :] = zeros
            if at:
                buf_uv[b, at + pad : at + pad + 8, :] = zeros[:8]
                buf_h[b, at + pad : at + pad + 8, :] = zeros[:8]
            buf_uv[b, at : at + wire, :] = uv
            buf_h[b, at : at + half, :] = hp
            buf_h[b, at + cells - half : at + cells, :] = other

    def halo_copy(t, side, g):
        return pltpu.make_async_remote_copy(
            src_ref=halo_send.at[t, side, g],
            dst_ref=halo_recv.at[t, side, g],
            send_sem=hsend_sem.at[t, side, g],
            recv_sem=hrecv_sem.at[t, side, g],
            device_id={"lat": band + 1 if side == 0 else band - 1},
            device_id_type=MESH,
        )

    def send_halos(t, g):
        south = jnp.zeros((pad, slab), jnp.float32)
        north = jnp.zeros((pad, slab), jnp.float32)
        for j in range(4):
            b = g * 4 + j
            h = cur_h[b, 8 : 8 + pad, :]
            vc = cur_uv[b, 8 : 8 + pad, :] * cosl
            at = 2 * width * j
            on_h = (lane >= at) & (lane < at + width)
            on_v = (lane >= at + width) & (lane < at + 2 * width)
            south = jnp.where(on_h, roll(h, at - (span - width)), south)
            south = jnp.where(on_v, roll(vc, at + width - (slab - width)), south)
            north = jnp.where(on_h, roll(h, at), north)
            north = jnp.where(on_v, roll(vc, at + width - span), north)
        halo_send[t, 0, g] = south
        halo_send[t, 1, g] = north

        @pl.when(has_south)
        def _():
            halo_copy(t, 0, g).start()

        @pl.when(has_north)
        def _():
            halo_copy(t, 1, g).start()

    def in1(k, _):
        g = lax.rem(my_group + k, groups)
        for j in range(4):
            b = g * 4 + j

            @pl.when(b != me)
            def _():
                copy1(b, b).wait_recv()

            unpack(b)
        send_halos(0, g)
        return 0

    lax.fori_loop(0, groups, in1, 0)

    def wrap_rows():
        def one(b, _):
            before = lax.rem(b + devs - 1, devs)
            after = lax.rem(b + 1, devs)
            for buf in (cur_uv, cur_h):
                buf[b, 7:8, :] = buf[before, 7 + cells : 8 + cells, :]
                buf[b, 8 + cells : 9 + cells, :] = buf[after, 8:9, :]
            return 0

        lax.fori_loop(0, devs, one, 0)

    def wait_halos(t, g):
        @pl.when(has_north)
        def _():
            halo_copy(t, 0, g).wait_recv()

        @pl.when(has_south)
        def _():
            halo_copy(t, 1, g).wait_recv()

    def tendencies(t):
        def group(k, _):
            g = lax.rem(my_group + k, groups)
            wait_halos(t, g)
            from_north = halo_recv[t, 0, g]
            from_south = halo_recv[t, 1, g]
            for j in range(4):
                b = g * 4 + j
                at = 2 * width * j
                uv = cur_uv[b, 8 : 8 + pad, :]
                h = cur_h[b, 8 : 8 + pad, :]
                duv = cur_uv[b, 9 : 9 + pad, :] - cur_uv[b, 7 : 7 + pad, :]
                dh = cur_h[b, 9 : 9 + pad, :] - cur_h[b, 7 : 7 + pad, :]
                vc = uv * cosl
                h_n = jnp.where(lane < width, roll(from_north, -at), roll(h, width))
                h_s = jnp.where(
                    lane >= span - width, roll(from_south, span - width - at), roll(h, -width)
                )
                v_n = jnp.where(
                    lane < span + width, roll(from_north, span - width - at), roll(vc, width)
                )
                v_s = jnp.where(
                    lane >= slab - width, roll(from_south, slab - 2 * width - at), roll(vc, -width)
                )
                mh = h_n - h_s
                mv = v_n - v_s
                tend_uv[b] = fcor * roll(uv, span) - k1 * jnp.where(low, dh, roll(mh, span))
                tend_h[b] = -(k2 * duv + k3 * roll(mv, span))
            return 0

        lax.fori_loop(0, groups, group, 0)

    def start_of(s):
        return 3 * part_pad * (s if s < 2 else 2 * s - 2)

    def put(s, half_at, j, piece, value):
        hi, lo = split(value)
        height = part_pad if s < 2 else 2 * part_pad
        at = start_of(s) + half_at * part_pad + j * pad
        columns = slice(piece * slab, (piece + 1) * slab)
        y_in[at : at + pad, columns] = hi
        y_in[at + height : at + height + pad, columns] = lo
        y_in[at + 2 * height : at + 2 * height + pad, columns] = hi

    def forward():
        for j in range(subs):
            for piece, buf in enumerate((tend_uv, tend_h)):
                x = [buf[g * subs + j] for g in range(RADIX)]
                a = [x[n] + x[n + 4] for n in range(4)]
                d = [x[n] - x[n + 4] for n in range(4)]
                plus, minus = a[0] + a[2], a[1] + a[3]
                put(0, 0, j, piece, plus + minus)
                put(1, 0, j, piece, plus - minus)
                less, more = ROOT * (d[1] - d[3]), ROOT * (d[1] + d[3])
                put(2, 0, j, piece, d[0] + less)
                put(2, 1, j, piece, -d[2] - more)
                put(3, 0, j, piece, a[0] - a[2])
                put(3, 1, j, piece, a[3] - a[1])
                put(4, 0, j, piece, d[0] - less)
                put(4, 1, j, piece, d[2] - more)

    def kept(wave, coefs):
        nearest = jnp.minimum(wave, points - wave).astype(jnp.float32)
        hi, lo = split(jnp.where(nearest <= cut, coefs, 0.0))
        return jnp.concatenate([hi, lo, hi], axis=0)

    def through():
        row = lax.broadcasted_iota(jnp.int32, (part_pad, 2 * slab), 0)
        mid = part // 2
        even = RADIX * jnp.where(row <= mid, row, row - mid)
        odd = RADIX * jnp.where(row < mid, row, row - mid) + RADIX // 2
        for s, wave in enumerate((even, odd)):
            at = pl.ds(s * part_pad, part_pad)
            coefs = dot(real_t[0, s], y_in[pl.ds(start_of(s), 3 * part_pad), :])
            y_out[at, :] = dot(real_t[1, s], kept(wave, coefs))
        both = lax.broadcasted_iota(jnp.int32, (2 * part_pad, 2 * slab), 0)
        wave8 = RADIX * jnp.where(both < part_pad, both, both - part_pad)

        for s in range(3):
            at = pl.ds((2 + 2 * s) * part_pad, 2 * part_pad)
            coefs = dot(mixed_t[0, s], y_in[pl.ds(start_of(s + 2), 6 * part_pad), :])
            y_out[at, :] = dot(mixed_t[1, s], kept(wave8 + (s + 1), coefs))

    def backward():
        for j in range(subs):
            for piece, buf in enumerate((tend_uv, tend_h)):
                y = [
                    y_out[pl.ds(n * part_pad + j * pad, pad), piece * slab : (piece + 1) * slab]
                    for n in range(RADIX)
                ]
                plus, minus = y[0] + y[1], y[0] - y[1]
                e, f = y[2] + y[6], y[7] - y[3]
                buf[0 * subs + j] = plus + y[4] + e
                buf[4 * subs + j] = plus + y[4] - e
                buf[2 * subs + j] = plus - y[4] + f
                buf[6 * subs + j] = plus - y[4] - f
                m, n = ROOT * (y[2] - y[6]), ROOT * (y[3] + y[7])
                buf[1 * subs + j] = minus - y[5] + (m - n)
                buf[5 * subs + j] = minus - y[5] - (m - n)
                buf[3 * subs + j] = minus + y[5] - (m + n)
                buf[7 * subs + j] = minus + y[5] + (m + n)

    quarter = rows * bands // 4
    filters = (band * rows < quarter) | (band * rows + rows > rows * bands - quarter)

    for t, (own, new) in enumerate(((0.0, 1.0), (0.75, 0.25), (1.0 / 3.0, 2.0 / 3.0))):
        wrap_rows()
        if t == 0:
            for copy in local[5:]:
                copy.wait()
        tendencies(t)

        @pl.when(filters)
        def _():
            forward()
            through()
            backward()

        def update(k, _):
            g = lax.rem(my_group + k, groups)
            for j in range(4):
                b = g * 4 + j
                for base, cur, tend in ((base_uv, cur_uv, tend_uv), (base_h, cur_h, tend_h)):
                    value = cur[b, 8 : 8 + pad, :] + tend[b]
                    if t > 0:
                        value = own * base[b] + new * value
                    cur[b, 8 : 8 + pad, :] = value
            send_halos(t + 1, g)
            return 0

        if t < 2:
            lax.fori_loop(0, groups, update, 0)

    def result(target, slot, b):
        def final(base, cur, tend, start, count):
            value = cur[b, 8 + start : 8 + start + count, :] + tend[b, start : start + count, :]
            return own * base[b, start : start + count, :] + new * value

        target[slot, 0:wire, :] = final(base_uv, cur_uv, tend_uv, 0, wire)
        h_first = final(base_h, cur_h, tend_h, 0, half)
        h_last = final(base_h, cur_h, tend_h, cells - half, half)
        target[slot, wire : wire + half, :] = jnp.where(low, h_first, roll(h_last, span))

    def out2(k, _):
        peer = lax.rem(me + k, devs)
        result(send2, peer, peer)
        copy2(peer, me).start()
        return 0

    lax.fori_loop(1, devs, out2, 0)
    result(recv2, me, me)

    def in2(k, _):
        peer = lax.rem(me + devs - k, devs)
        copy2(peer, peer).wait_recv()
        return 0

    lax.fori_loop(1, devs, in2, 0)

    def wide(value):
        if slab == levels:
            return value
        fill_up = jnp.zeros((value.shape[0], levels - slab), jnp.float32)
        return jnp.concatenate([value, fill_up], axis=1)

    outs = (u_out, v_out, h_out)

    def gathered(n, first, count):
        total = jnp.zeros((count, levels), jnp.float32)
        here = lane_lev[:count]
        for d in range(devs):
            piece = wide(recv2[d, first : first + count, :])
            piece = pltpu.roll(piece, (d - n) * width % levels, 1)
            total = jnp.where((here >= d * width) & (here < (d + 1) * width), piece, total)
        return total

    for n in range(2 * rows):
        ref = outs[n // rows]
        ref[pl.ds(n % rows, cells, stride=rows), :] = gathered(n, 0, cells)
        start = (n // rows) * (cells - half)
        h_out[pl.ds(n % rows + rows * start, half, stride=rows), :] = gathered(n, wire, half)

    def done(k, _):
        peer = lax.rem(me + k, devs)
        copy1(peer, me).wait_send()
        copy2(peer, me).wait_send()
        return 0

    lax.fori_loop(1, devs, done, 0)

    for t in range(3):
        for g in range(groups):
            @pl.when(has_south)
            def _():
                halo_copy(t, 0, g).wait_send()

            @pl.when(has_north)
            def _():
                halo_copy(t, 1, g).wait_send()


def shards(geo_tab, real_tab, mixed_tab, bands, devs, pad, u_wind, v_wind, height, wave_speed, cutoff):
    cells, rows, levels = u_wind.shape
    width = levels // devs
    slab = 2 * rows * width
    wire = round_up(cells, 8)
    half = round_up(-(-cells // 2), 8)
    f32, bf16 = jnp.float32, jnp.bfloat16
    part_pad = devs // RADIX * pad
    dims = (bands, devs, cells, rows, width, pad, wire, half)
    vmem = pl.BlockSpec(memory_space=pltpu.VMEM)
    anywhere = pl.BlockSpec(memory_space=pl.ANY)
    flat = jax.ShapeDtypeStruct((cells * rows, levels), f32)
    dma = pltpu.SemaphoreType.DMA
    outs = pl.pallas_call(
        functools.partial(kernel, dims),
        out_shape=(flat, flat, flat),
        in_specs=[anywhere] * 4 + [pl.BlockSpec(memory_space=pltpu.SMEM)] + [anywhere] * 3,
        out_specs=(vmem, vmem, vmem),
        scratch_shapes=[
            pltpu.VMEM(flat.shape, f32),
            pltpu.VMEM(flat.shape, f32),
            pltpu.VMEM(flat.shape, f32),
            pltpu.VMEM((1, levels), f32),
            pltpu.VMEM(geo_tab.shape, f32),
            pltpu.VMEM(real_tab.shape, bf16),
            pltpu.VMEM(mixed_tab.shape, bf16),
            pltpu.VMEM((devs, wire + half, slab), f32),
            pltpu.VMEM((devs, wire + half, slab), f32),
            pltpu.VMEM((devs, wire + half, slab), f32),
            pltpu.VMEM((devs, wire + half, slab), f32),
            pltpu.VMEM((devs, pad, slab), f32),
            pltpu.VMEM((devs, pad, slab), f32),
            pltpu.VMEM((devs, pad + 16, slab), f32),
            pltpu.VMEM((devs, pad + 16, slab), f32),
            pltpu.VMEM((devs, pad, slab), f32),
            pltpu.VMEM((devs, pad, slab), f32),
            pltpu.VMEM((3 * RADIX * part_pad, 2 * slab), bf16),
            pltpu.VMEM((RADIX * part_pad, 2 * slab), f32),
            pltpu.VMEM((3, 2, devs // 4, pad, slab), f32),
            pltpu.VMEM((3, 2, devs // 4, pad, slab), f32),
            dma((7,)),
            dma((devs,)),
            dma((devs,)),
            dma((devs,)),
            dma((devs,)),
            dma((3, 2, devs // 4)),
            dma((3, 2, devs // 4)),
        ],
        compiler_params=pltpu.CompilerParams(
            collective_id=0, has_side_effects=True, vmem_limit_bytes=48 * 1024 * 1024
        ),
    )(
        u_wind.reshape(cells * rows, levels),
        v_wind.reshape(cells * rows, levels),
        height.reshape(cells * rows, levels),
        wave_speed.reshape(1, levels),
        cutoff,
        jnp.asarray(geo_tab),
        jnp.asarray(real_tab),
        jnp.asarray(mixed_tab),
    )
    return tuple(out.reshape(cells, rows, levels) for out in outs)


def solution(mesh):
    bands, devs = mesh.shape["lat"], mesh.shape["lon"]

    def step(u_wind, v_wind, height, wave_speed, cutoff):
        points = u_wind.shape[0]
        pad = round_up(points // devs + 1, 16)
        real_tab, mixed_tab = tables(points, points // devs, pad)
        rows, width = u_wind.shape[1] // bands, u_wind.shape[2] // devs
        geo_tab = geometry(points, bands, rows, width)
        spec = P("lon", "lat", None)
        local = functools.partial(shards, geo_tab, real_tab, mixed_tab, bands, devs, pad)
        return jax.shard_map(
            local,
            mesh=mesh,
            in_specs=(spec, spec, spec, P(), P()),
            out_specs=(spec, spec, spec),
            check_vma=False,
        )(u_wind, v_wind, height, wave_speed, cutoff)

    return step
```

time: 663 us -> 72.1 us (0.11)
  the two profiles are of different devices: /device:TPU:0 before, /device:TPU:3 now
where the time goes in v1:
time: 72.1 us; the launch traced here: 71.8 us
  Pallas kernels  62.7 us (87%)
  local copies, waits for them, and re-layouts  8.4 us (12%)
    pallas_call x1, Pallas kernels, shards(): pl.pallas_call(functools.partial(kernel, dims), out_shape=(flat, flat, fl...  62.7 us
    unnamed x17, local copies, waits for them, and re-layouts  8.4 us

profile of v1, /device:TPU:3, one launch (start us, length us, event | category | flops | bytes accessed | tf_op | source)
XLA Modules:
  0.0 71.8 jit_solution(17427036182949314549)
XLA Ops:
  0.6 0.0 copy-start
  0.6 1.2 %copy-done = bf16[2,2,192,576]{3,2,1,0:T(8,128)(2,1)S(1)} copy-done((bf16[2,2,192,576]{3,2,1,0:T(8,128)(2,1)S(1)}, bf16[2,2,192,576]{3,2,1,0:T(8,128)(2,1)}, u32[]{:S(2)}) %copy-start) | copy-done | bytes 884760
  1.8 0.0 copy-start.1
  1.8 1.0 %copy-done.1 = f32[180,4,128]{2,1,0:T(4,128)S(1)} copy-done((f32[180,4,128]{2,1,0:T(4,128)S(1)}, f32[180,4,128]{2,1,0:T(4,128)}, u32[]{:S(2)}) %copy-start.1) | copy-done | bytes 368664
  2.8 0.0 copy-start.2
  2.8 1.0 %copy-done.2 = f32[180,4,128]{2,1,0:T(4,128)S(1)} copy-done((f32[180,4,128]{2,1,0:T(4,128)S(1)}, f32[180,4,128]{2,1,0:T(4,128)}, u32[]{:S(2)}) %copy-start.2) | copy-done | bytes 368664
  3.8 0.0 copy-start.3
  3.8 1.0 %copy-done.3 = f32[180,4,128]{2,1,0:T(4,128)S(1)} copy-done((f32[180,4,128]{2,1,0:T(4,128)S(1)}, f32[180,4,128]{2,1,0:T(4,128)}, u32[]{:S(2)}) %copy-start.3) | copy-done | bytes 368664
  4.8 0.0 copy-start.4
  4.8 0.7 copy-done.4
  5.5 0.0 copy-start.5
  5.5 0.7 copy-done.5
  6.2 0.0 copy-start.6
  6.2 0.7 copy-done.6
  6.8 62.7 %shard_map.103 = (f32[720,128]{1,0:T(8,128)S(1)}, f32[720,128]{1,0:T(8,128)S(1)}, f32[720,128]{1,0:T(8,128)S(1)}) custom-call(f32[720,128]{1,0:T(8,128)S(1)} %bitcast.7, f32[720,128]{1,0:T(8,128)S(1)} %bitcast.8, f32[720,128]{1,0:T(8,128)S(1)} %bitcast.9, f32[1,128]{1,0:T(1,128)S(1)} %bitcast.13, s32[16]{0:T(128)S(1)} %copy-done.6, f32[32,128]{1,0:T(8,128)S(1)} %copy-done.4, ...), custom_call_target="tpu_custom_call" | custom-call | tf_op jit(solution)/shard_map/pallas_call | solution.py:583
  69.6 0.7 %copy.14 = f32[180,4,128]{2,1,0:T(4,128)} copy(f32[180,4,128]{2,1,0:T(4,128)S(1)} %bitcast.12) | data formatting | bytes 737280
  70.3 0.7 %copy.15 = f32[180,4,128]{2,1,0:T(4,128)} copy(f32[180,4,128]{2,1,0:T(4,128)S(1)} %bitcast.11) | data formatting | bytes 737280
  71.0 0.7 %copy.16 = f32[180,4,128]{2,1,0:T(4,128)} copy(f32[180,4,128]{2,1,0:T(4,128)S(1)} %bitcast.10) | data formatting | bytes 737280
Async XLA Ops:
  0.6 1.2 %copy-start = (bf16[2,2,192,576]{3,2,1,0:T(8,128)(2,1)S(1)}, bf16[2,2,192,576]{3,2,1,0:T(8,128)(2,1)}, u32[]{:S(2)}) copy-start(bf16[2,2,192,576]{3,2,1,0:T(8,128)(2,1)} %constant.7.clone.real_hbm) | copy-start | bytes 2654212
  1.8 1.0 %copy-start.1 = (f32[180,4,128]{2,1,0:T(4,128)S(1)}, f32[180,4,128]{2,1,0:T(4,128)}, u32[]{:S(2)}) copy-start(f32[180,4,128]{2,1,0:T(4,128)} %param.8) | copy-start | bytes 1105924
  2.8 1.0 %copy-start.2 = (f32[180,4,128]{2,1,0:T(4,128)S(1)}, f32[180,4,128]{2,1,0:T(4,128)}, u32[]{:S(2)}) copy-start(f32[180,4,128]{2,1,0:T(4,128)} %param.9) | copy-start | bytes 1105924
  3.8 1.0 %copy-start.3 = (f32[180,4,128]{2,1,0:T(4,128)S(1)}, f32[180,4,128]{2,1,0:T(4,128)}, u32[]{:S(2)}) copy-start(f32[180,4,128]{2,1,0:T(4,128)} %param.10) | copy-start | bytes 1105924
  4.8 0.7 copy-start.4
  5.5 0.7 copy-start.5
  6.2 0.7 copy-start.6

commit v2 on v1

--- a/solution.py
+++ b/solution.py
@@ -240,8 +240,18 @@
             device_id_type=MESH,
         )
 
+    def partner(k):
+        k = devs - k
+        if devs & (devs - 1):
+            return lax.rem(me + k, devs)
+        peer, bit = 0, 1
+        while bit < devs:
+            peer = peer + bit * ((me // bit + k // bit) % 2)
+            bit *= 2
+        return peer
+
     def out1(k, _):
-        peer = lax.rem(me + k, devs)
+        peer = partner(k)
         fill(send1, peer, peer)
         copy1(peer, me).start()
         return 0
@@ -366,34 +376,39 @@
         def _():
             halo_copy(t, 1, g).wait_recv()
 
+    chunk = 48 if pad % 48 == 0 else 16
+
+    def tendency(b, top, at, from_north, from_south):
+        uv = cur_uv[b, 8 + top : 8 + top + chunk, :]
+        h = cur_h[b, 8 + top : 8 + top + chunk, :]
+        duv = cur_uv[b, 9 + top : 9 + top + chunk, :] - cur_uv[b, 7 + top : 7 + top + chunk, :]
+        dh = cur_h[b, 9 + top : 9 + top + chunk, :] - cur_h[b, 7 + top : 7 + top + chunk, :]
+        vc = uv * cosl
+        h_n = jnp.where(lane < width, roll(from_north, -at), roll(h, width))
+        h_s = jnp.where(
+            lane >= span - width, roll(from_south, span - width - at), roll(h, -width)
+        )
+        v_n = jnp.where(
+            lane < span + width, roll(from_north, span - width - at), roll(vc, width)
+        )
+        v_s = jnp.where(
+            lane >= slab - width, roll(from_south, slab - 2 * width - at), roll(vc, -width)
+        )
+        mh = h_n - h_s
+        mv = v_n - v_s
+        tend_uv[b, top : top + chunk, :] = fcor * roll(uv, span) - k1 * jnp.where(low, dh, roll(mh, span))
+        tend_h[b, top : top + chunk, :] = -(k2 * duv + k3 * roll(mv, span))
+
     def tendencies(t):
         def group(k, _):
             g = lax.rem(my_group + k, groups)
             wait_halos(t, g)
-            from_north = halo_recv[t, 0, g]
-            from_south = halo_recv[t, 1, g]
             for j in range(4):
                 b = g * 4 + j
                 at = 2 * width * j
-                uv = cur_uv[b, 8 : 8 + pad, :]
-                h = cur_h[b, 8 : 8 + pad, :]
-                duv = cur_uv[b, 9 : 9 + pad, :] - cur_uv[b, 7 : 7 + pad, :]
-                dh = cur_h[b, 9 : 9 + pad, :] - cur_h[b, 7 : 7 + pad, :]
-                vc = uv * cosl
-                h_n = jnp.where(lane < width, roll(from_north, -at), roll(h, width))
-                h_s = jnp.where(
-                    lane >= span - width, roll(from_south, span - width - at), roll(h, -width)
-                )
-                v_n = jnp.where(
-                    lane < span + width, roll(from_north, span - width - at), roll(vc, width)
-                )
-                v_s = jnp.where(
-                    lane >= slab - width, roll(from_south, slab - 2 * width - at), roll(vc, -width)
-                )
-                mh = h_n - h_s
-                mv = v_n - v_s
-                tend_uv[b] = fcor * roll(uv, span) - k1 * jnp.where(low, dh, roll(mh, span))
-                tend_h[b] = -(k2 * duv + k3 * roll(mv, span))
+                for top in range(0, pad, chunk):
+                    tendency(b, top, at, halo_recv[t, 0, g, top : top + chunk, :],
+                             halo_recv[t, 1, g, top : top + chunk, :])
             return 0
 
         lax.fori_loop(0, groups, group, 0)
@@ -401,31 +416,38 @@
     def start_of(s):
         return 3 * part_pad * (s if s < 2 else 2 * s - 2)
 
-    def put(s, half_at, j, piece, value):
+    def put(s, half_at, j, top, piece, value):
         hi, lo = split(value)
         height = part_pad if s < 2 else 2 * part_pad
         at = start_of(s) + half_at * part_pad + j * pad
         columns = slice(piece * slab, (piece + 1) * slab)
-        y_in[at : at + pad, columns] = hi
-        y_in[at + height : at + height + pad, columns] = lo
-        y_in[at + 2 * height : at + 2 * height + pad, columns] = hi
-
-    def forward():
+        for n, part_of in enumerate((hi, lo, hi)):
+            spot = pl.ds(pl.multiple_of(at + n * height + top, 16), 16)
+            y_in[spot, columns] = part_of
+
+    def each_chunk(body):
+        def one(n, _):
+            body(pl.multiple_of(n * 16, 16))
+            return 0
+
+        lax.fori_loop(0, pad // 16, one, 0)
+
+    def forward(top):
         for j in range(subs):
             for piece, buf in enumerate((tend_uv, tend_h)):
-                x = [buf[g * subs + j] for g in range(RADIX)]
+                x = [buf[g * subs + j, pl.ds(top, 16), :] for g in range(RADIX)]
                 a = [x[n] + x[n + 4] for n in range(4)]
                 d = [x[n] - x[n + 4] for n in range(4)]
                 plus, minus = a[0] + a[2], a[1] + a[3]
-                put(0, 0, j, piece, plus + minus)
-                put(1, 0, j, piece, plus - minus)
+                put(0, 0, j, top, piece, plus + minus)
+                put(1, 0, j, top, piece, plus - minus)
                 less, more = ROOT * (d[1] - d[3]), ROOT * (d[1] + d[3])
-                put(2, 0, j, piece, d[0] + less)
-                put(2, 1, j, piece, -d[2] - more)
-                put(3, 0, j, piece, a[0] - a[2])
-                put(3, 1, j, piece, a[3] - a[1])
-                put(4, 0, j, piece, d[0] - less)
-                put(4, 1, j, piece, d[2] - more)
+                put(2, 0, j, top, piece, d[0] + less)
+                put(2, 1, j, top, piece, -d[2] - more)
+                put(3, 0, j, top, piece, a[0] - a[2])
+                put(3, 1, j, top, piece, a[3] - a[1])
+                put(4, 0, j, top, piece, d[0] - less)
+                put(4, 1, j, top, piece, d[2] - more)
 
     def kept(wave, coefs):
         nearest = jnp.minimum(wave, points - wave).astype(jnp.float32)
@@ -449,24 +471,24 @@
             coefs = dot(mixed_t[0, s], y_in[pl.ds(start_of(s + 2), 6 * part_pad), :])
             y_out[at, :] = dot(mixed_t[1, s], kept(wave8 + (s + 1), coefs))
 
-    def backward():
+    def backward(top):
         for j in range(subs):
             for piece, buf in enumerate((tend_uv, tend_h)):
                 y = [
-                    y_out[pl.ds(n * part_pad + j * pad, pad), piece * slab : (piece + 1) * slab]
+                    y_out[pl.ds(pl.multiple_of(n * part_pad + j * pad + top, 16), 16), piece * slab : (piece + 1) * slab]
                     for n in range(RADIX)
                 ]
                 plus, minus = y[0] + y[1], y[0] - y[1]
                 e, f = y[2] + y[6], y[7] - y[3]
-                buf[0 * subs + j] = plus + y[4] + e
-                buf[4 * subs + j] = plus + y[4] - e
-                buf[2 * subs + j] = plus - y[4] + f
-                buf[6 * subs + j] = plus - y[4] - f
+                buf[0 * subs + j, pl.ds(top, 16), :] = plus + y[4] + e
+                buf[4 * subs + j, pl.ds(top, 16), :] = plus + y[4] - e
+                buf[2 * subs + j, pl.ds(top, 16), :] = plus - y[4] + f
+                buf[6 * subs + j, pl.ds(top, 16), :] = plus - y[4] - f
                 m, n = ROOT * (y[2] - y[6]), ROOT * (y[3] + y[7])
-                buf[1 * subs + j] = minus - y[5] + (m - n)
-                buf[5 * subs + j] = minus - y[5] - (m - n)
-                buf[3 * subs + j] = minus + y[5] - (m + n)
-                buf[7 * subs + j] = minus + y[5] + (m + n)
+                buf[1 * subs + j, pl.ds(top, 16), :] = minus - y[5] + (m - n)
+                buf[5 * subs + j, pl.ds(top, 16), :] = minus - y[5] - (m - n)
+                buf[3 * subs + j, pl.ds(top, 16), :] = minus + y[5] - (m + n)
+                buf[7 * subs + j, pl.ds(top, 16), :] = minus + y[5] + (m + n)
 
     quarter = rows * bands // 4
     filters = (band * rows < quarter) | (band * rows + rows > rows * bands - quarter)
@@ -480,9 +502,9 @@
 
         @pl.when(filters)
         def _():
-            forward()
+            each_chunk(forward)
             through()
-            backward()
+            each_chunk(backward)
 
         def update(k, _):
             g = lax.rem(my_group + k, groups)
@@ -510,7 +532,7 @@
         target[slot, wire : wire + half, :] = jnp.where(low, h_first, roll(h_last, span))
 
     def out2(k, _):
-        peer = lax.rem(me + k, devs)
+        peer = partner(k)
         result(send2, peer, peer)
         copy2(peer, me).start()
         return 0
@@ -577,7 +599,7 @@
     part_pad = devs // RADIX * pad
     dims = (bands, devs, cells, rows, width, pad, wire, half)
     vmem = pl.BlockSpec(memory_space=pltpu.VMEM)
-    anywhere = pl.BlockSpec(memory_space=pl.ANY)
+    anywhere = pl.BlockSpec(memory_space=pltpu.HBM)
     flat = jax.ShapeDtypeStruct((cells * rows, levels), f32)
     dma = pltpu.SemaphoreType.DMA
     outs = pl.pallas_call(

time: 72.1 us -> 75.2 us (1.043)
  the two profiles are of different devices: /device:TPU:3 before, /device:TPU:0 now
where the time goes in v2:
time: 75.2 us; the launch traced here: 74.8 us
  Pallas kernels  65.8 us (88%)
  local copies, waits for them, and re-layouts  8.4 us (11%)
    pallas_call x1, Pallas kernels, shards(): pl.pallas_call(functools.partial(kernel, dims), out_shape=(flat, flat, fl...  65.8 us
    unnamed x17, local copies, waits for them, and re-layouts  8.4 us

profile of v2, /device:TPU:0, one launch (start us, length us, event | category | flops | bytes accessed | tf_op | source)
XLA Modules:
  0.0 74.8 jit_solution(12024797389296936453)
XLA Ops:
  0.6 0.0 copy-start
  0.6 1.2 %copy-done = bf16[2,2,192,576]{3,2,1,0:T(8,128)(2,1)S(1)} copy-done((bf16[2,2,192,576]{3,2,1,0:T(8,128)(2,1)S(1)}, bf16[2,2,192,576]{3,2,1,0:T(8,128)(2,1)}, u32[]{:S(2)}) %copy-start) | copy-done | bytes 884760
  1.8 0.0 copy-start.1
  1.8 1.0 %copy-done.1 = f32[180,4,128]{2,1,0:T(4,128)S(1)} copy-done((f32[180,4,128]{2,1,0:T(4,128)S(1)}, f32[180,4,128]{2,1,0:T(4,128)}, u32[]{:S(2)}) %copy-start.1) | copy-done | bytes 368664
  2.8 0.0 copy-start.2
  2.8 1.0 %copy-done.2 = f32[180,4,128]{2,1,0:T(4,128)S(1)} copy-done((f32[180,4,128]{2,1,0:T(4,128)S(1)}, f32[180,4,128]{2,1,0:T(4,128)}, u32[]{:S(2)}) %copy-start.2) | copy-done | bytes 368664
  3.8 0.0 copy-start.3
  3.8 1.0 %copy-done.3 = f32[180,4,128]{2,1,0:T(4,128)S(1)} copy-done((f32[180,4,128]{2,1,0:T(4,128)S(1)}, f32[180,4,128]{2,1,0:T(4,128)}, u32[]{:S(2)}) %copy-start.3) | copy-done | bytes 368664
  4.8 0.0 copy-start.4
  4.8 0.7 copy-done.4
  5.5 0.0 copy-start.5
  5.5 0.7 copy-done.5
  6.2 0.0 copy-start.6
  6.2 0.7 copy-done.6
  6.8 65.8 %shard_map.103 = (f32[720,128]{1,0:T(8,128)S(1)}, f32[720,128]{1,0:T(8,128)S(1)}, f32[720,128]{1,0:T(8,128)S(1)}) custom-call(f32[720,128]{1,0:T(8,128)S(1)} %bitcast.7, f32[720,128]{1,0:T(8,128)S(1)} %bitcast.8, f32[720,128]{1,0:T(8,128)S(1)} %bitcast.9, f32[1,128]{1,0:T(1,128)S(1)} %bitcast.13, s32[16]{0:T(128)S(1)} %copy-done.6, f32[32,128]{1,0:T(8,128)S(1)} %copy-done.4, ...), custom_call_target="tpu_custom_call" | custom-call | tf_op jit(solution)/shard_map/pallas_call | solution.py:605
  72.6 0.7 copy.14
  73.4 0.7 copy.15
  74.1 0.7 copy.16
Async XLA Ops:
  0.6 1.2 %copy-start = (bf16[2,2,192,576]{3,2,1,0:T(8,128)(2,1)S(1)}, bf16[2,2,192,576]{3,2,1,0:T(8,128)(2,1)}, u32[]{:S(2)}) copy-start(bf16[2,2,192,576]{3,2,1,0:T(8,128)(2,1)} %constant.7.clone.real_hbm) | copy-start | bytes 2654212
  1.8 1.0 %copy-start.1 = (f32[180,4,128]{2,1,0:T(4,128)S(1)}, f32[180,4,128]{2,1,0:T(4,128)}, u32[]{:S(2)}) copy-start(f32[180,4,128]{2,1,0:T(4,128)} %param.8) | copy-start | bytes 1105924
  2.8 1.0 %copy-start.2 = (f32[180,4,128]{2,1,0:T(4,128)S(1)}, f32[180,4,128]{2,1,0:T(4,128)}, u32[]{:S(2)}) copy-start(f32[180,4,128]{2,1,0:T(4,128)} %param.9) | copy-start | bytes 1105924
  3.8 1.0 %copy-start.3 = (f32[180,4,128]{2,1,0:T(4,128)S(1)}, f32[180,4,128]{2,1,0:T(4,128)}, u32[]{:S(2)}) copy-start(f32[180,4,128]{2,1,0:T(4,128)} %param.10) | copy-start | bytes 1105924
  4.8 0.7 copy-start.4
  5.5 0.7 copy-start.5
  6.2 0.7 copy-start.6
